TPU v7x, 256 devices: a whole 4x4x8 slice. The times are simulated.
256 devices in a mesh: ctx: 64 (over z, y, core), tsp: 4 (over x).
Axes of the slice: x: 4, y: 4, z: 8, core: 2. Of those that a mesh axis runs over, the one named last changes fastest.
Arguments:
- queries: bfloat16 [32768, 5120], P(('ctx', 'tsp')), may hold values from -6 to 6
- keys: bfloat16 [32768, 5120], P(('ctx', 'tsp')), may hold values from -6 to 6
- values: bfloat16 [32768, 5120], P(('ctx', 'tsp')), may hold values from -6 to 6
- cotangent: bfloat16 [32768, 5120], P(('ctx', 'tsp')), may hold values from -6 to 6
- content_bias: float32 [40, 128], P('tsp'), may hold values from -5 to 5
- memory_lengths: int32 [64], P('ctx'), may hold values from 0 to 1536, as said below
- segment_ends: int32 [64], P('ctx'), may hold values from 1 to 512, as said below
Outputs:
- attended: bfloat16 [32768, 5120], P(('ctx', 'tsp'))
- grad_queries: bfloat16 [32768, 5120], P(('ctx', 'tsp'))
- grad_keys: bfloat16 [32768, 5120], P(('ctx', 'tsp'))
- grad_values: bfloat16 [32768, 5120], P(('ctx', 'tsp'))
- grad_bias: float32 [40, 128], P('tsp')
Inputs may be any that keep to these rules, and one draw needn't show every extreme that they name: memory_lengths[0] is 0 and the last shard's value is 1536. `segment_ends`: a value of 512 means that the shard's first document runs to its end; shard 1 has the value 1 and the last shard the value 512.
All inputs are finite; a program needn't handle non-finite values.
Results may differ from a plain program's by a relative error of at most 0.012.
The roundings to bfloat16 on the way count: a program that leaves them out, or rounds other values in their place, can miss the bound.
Values may be sent and summed in bfloat16 or wider, within the bound.
A program may use at most 128 MiB of HBM per device.

v0:
```python
import math

import jax
import jax.numpy as jnp
from jax import lax
from jax.sharding import PartitionSpec as P

MEM = 1536


def passed_along(value, axis, steps):
    count = lax.axis_size(axis)
    initial, last = (max(0, -steps), min(count, count - steps))
    return lax.ppermute(value, axis, [(source, source + steps) for source in range(initial, last)])


def column_block(matrix, first_col, count):
    return lax.dynamic_slice_in_dim(matrix, first_col, count, 1)


def merge_heads(piece_stack):
    head_total, tok_rows, head_size = piece_stack.shape
    return jnp.transpose(piece_stack, (1, 0, 2)).reshape(tok_rows, head_total * head_size)


def shards(queries, keys, values, cotangent, content_bias, memory_lengths, segment_ends):
    q_heads, k_heads, v_heads, g_heads = (
        lax.all_to_all(queries, "tsp", split_axis=1, concat_axis=0, tiled=True),
        lax.all_to_all(keys, "tsp", split_axis=1, concat_axis=0, tiled=True),
        lax.all_to_all(values, "tsp", split_axis=1, concat_axis=0, tiled=True),
        lax.all_to_all(cotangent, "tsp", split_axis=1, concat_axis=0, tiled=True),
    )
    tok_rows = q_heads.shape[0]
    local_heads = content_bias.shape[0]
    head_size = content_bias.shape[1]
    shard_count = (MEM + tok_rows - 1) // tok_rows
    stacked = jnp.stack([k_heads, v_heads])
    blocks = []
    current = stacked
    for stride in range(shard_count):
        current = passed_along(current, "ctx", 1)
        blocks = [current] + blocks
    window = jnp.concatenate(blocks, axis=1)
    position = lax.axis_index("ctx")
    usable = jnp.minimum(memory_lengths[0], position * tok_rows)
    boundary = segment_ends[0]
    span_rows = MEM + tok_rows
    row_index = lax.broadcasted_iota(jnp.int32, (tok_rows, span_rows), 0)
    col_index = lax.broadcasted_iota(jnp.int32, (tok_rows, span_rows), 1)
    offset = col_index - MEM
    memory_ok = (col_index < MEM) & (col_index >= MEM - usable) & (row_index < boundary)
    local_ok = (
        (col_index >= MEM) & (offset <= row_index) & ((row_index < boundary) == (offset < boundary))
    )
    allowed = memory_ok | local_ok
    scaling = 1.0 / math.sqrt(head_size)
    contract_cols = (((1,), (1,)), ((), ()))
    contract_rows = (((0,), (0,)), ((), ()))

    def one_head(head_index):
        first_col = head_index * head_size
        query_rows = column_block(q_heads, first_col, head_size)
        head_bias = lax.dynamic_slice_in_dim(content_bias, head_index, 1, 0)
        shifted = (query_rows.astype(jnp.float32) + head_bias).astype(jnp.bfloat16)
        key_rows = jnp.concatenate(
            [
                column_block(window[0], first_col, head_size),
                column_block(k_heads, first_col, head_size),
            ],
            axis=0,
        )
        value_rows = jnp.concatenate(
            [
                column_block(window[1], first_col, head_size),
                column_block(v_heads, first_col, head_size),
            ],
            axis=0,
        )
        grad_rows = column_block(g_heads, first_col, head_size)
        scores = (
            lax.dot_general(shifted, key_rows, contract_cols, preferred_element_type=jnp.float32)
            * scaling
        )
        scores = jnp.where(allowed, scores, -jnp.inf)
        row_peak = jnp.max(scores, axis=1, keepdims=True)
        weights = jnp.exp(scores - row_peak)
        probs_full = weights / jnp.sum(weights, axis=1, keepdims=True)
        probs_half = probs_full.astype(jnp.bfloat16)
        attended = jnp.dot(probs_half, value_rows, preferred_element_type=jnp.float32).astype(
            jnp.bfloat16
        )
        grad_probs = lax.dot_general(
            grad_rows, value_rows, contract_cols, preferred_element_type=jnp.float32
        )
        centre = jnp.sum(probs_full * grad_probs, axis=1, keepdims=True)
        grad_scores = (probs_full * (grad_probs - centre) * scaling).astype(jnp.bfloat16)
        grad_query = jnp.dot(grad_scores, key_rows, preferred_element_type=jnp.float32)
        grad_key = lax.dot_general(
            grad_scores[:, MEM:], shifted, contract_rows, preferred_element_type=jnp.float32
        ).astype(jnp.bfloat16)
        grad_value = lax.dot_general(
            probs_half[:, MEM:], grad_rows, contract_rows, preferred_element_type=jnp.float32
        ).astype(jnp.bfloat16)
        return (
            attended,
            grad_query.astype(jnp.bfloat16),
            grad_key,
            grad_value,
            jnp.sum(grad_query, axis=0),
        )

    results = lax.map(one_head, jnp.arange(local_heads, dtype=jnp.int32))
    attended = merge_heads(results[0])
    grad_queries = merge_heads(results[1])
    grad_keys = merge_heads(results[2])
    grad_values = merge_heads(results[3])
    grad_bias = lax.psum(results[4], "ctx")
    outputs = (
        lax.all_to_all(attended, "tsp", split_axis=0, concat_axis=1, tiled=True),
        lax.all_to_all(grad_queries, "tsp", split_axis=0, concat_axis=1, tiled=True),
        lax.all_to_all(grad_keys, "tsp", split_axis=0, concat_axis=1, tiled=True),
        lax.all_to_all(grad_values, "tsp", split_axis=0, concat_axis=1, tiled=True),
    )
    return (outputs[0], outputs[1], outputs[2], outputs[3], grad_bias)


def solution(mesh):
    return jax.shard_map(
        shards,
        mesh=mesh,
        in_specs=(
            P(("ctx", "tsp"), None),
            P(("ctx", "tsp"), None),
            P(("ctx", "tsp"), None),
            P(("ctx", "tsp"), None),
            P("tsp", None),
            P("ctx"),
            P("ctx"),
        ),
        out_specs=(
            P(("ctx", "tsp"), None),
            P(("ctx", "tsp"), None),
            P(("ctx", "tsp"), None),
            P(("ctx", "tsp"), None),
            P("tsp", None),
        ),
        check_vma=False,
    )
```

profile of v0, /device:TPU:1, one launch (start us, length us, event | category | flops | bytes accessed | tf_op | source)
XLA Modules:
  0.0 595.5 jit_solution(16991121875115040467)
XLA Ops:
  3.2 4.8 all-to-all-start.1
  8.1 15.4 %all-to-all-done.1 = bf16[128,4,1280]{2,0,1:T(8,128)(2,1)} async-done(((bf16[128,4,1280]{2,0,1:T(8,128)(2,1)}), bf16[128,4,1280]{2,0,1:T(8,128)(2,1)}, u32[]{:S(2)}, u32[]{:S(2)}) %all-to-all-start.1) | async-done | bytes 1310752 | tf_op jit(solution)/shard_map/all_to_all | solution.py:29
  23.5 17.3 %all_to_all.152 = bf16[128,4,1280]{2,0,1:T(8,128)(2,1)} all-to-all(bf16[128,4,1280]{2,0,1:T(8,128)(2,1)S(1)} %bitcast.107), channel_id=1, replica_groups=mesh['ctx'=64,'tsp'=4] {'tsp'}, dimensions={1} | all-to-all | bytes 2621440 | tf_op jit(solution)/shard_map/all_to_all | solution.py:30
  42.8 10.0 %collective-permute-start = (bf16[2,512,1280]{2,1,0:T(8,128)(2,1)S(1)}, bf16[2,512,1280]{2,1,0:T(8,128)(2,1)S(1)}, u32[]{:S(2)}, u32[]{:S(2)}) collective-permute-start(bf16[2,512,1280]{2,1,0:T(8,128)(2,1)S(1)} %pad_maximum_fusion.7), channel_id=1, source_target_pairs={{0,4},{4,8},{8,12},{12,16},{16,20},{20,24},{24,28},{28,32},{32,36}... | collective-permute-start | bytes 7864328 | tf_op jit(solution)/shard_map/ppermute | solution.py:14
  52.9 28.6 %collective-permute-done = bf16[2,512,1280]{2,1,0:T(8,128)(2,1)S(1)} collective-permute-done((bf16[2,512,1280]{2,1,0:T(8,128)(2,1)S(1)}, bf16[2,512,1280]{2,1,0:T(8,128)(2,1)S(1)}, u32[]{:S(2)}, u32[]{:S(2)}) %collective-permute-start) | collective-permute-done | bytes 2621472 | tf_op jit(solution)/shard_map/ppermute | solution.py:14
  81.4 4.4 collective-permute-start.1
  85.8 28.6 %collective-permute-done.1 = bf16[2,512,1280]{2,1,0:T(8,128)(2,1)} collective-permute-done((bf16[2,512,1280]{2,1,0:T(8,128)(2,1)S(1)}, bf16[2,512,1280]{2,1,0:T(8,128)(2,1)}, u32[]{:S(2)}, u32[]{:S(2)}) %collective-permute-start.1) | collective-permute-done | bytes 2621472 | tf_op jit(solution)/shard_map/ppermute | solution.py:14
  114.4 4.5 collective-permute-start.2
  120.1 4.3 all-to-all-start
  128.3 14.5 %all-to-all-done = bf16[128,4,1280]{2,0,1:T(8,128)(2,1)} async-done(((bf16[128,4,1280]{2,0,1:T(8,128)(2,1)}), bf16[128,4,1280]{2,0,1:T(8,128)(2,1)}, u32[]{:S(2)}, u32[]{:S(2)}) %all-to-all-start) | async-done | bytes 1310752 | tf_op jit(solution)/shard_map/all_to_all | solution.py:28
  142.8 4.3 all-to-all-start.3
  147.8 6.2 %pad_maximum_fusion.6 = bf16[2,1536,1280]{2,1,0:T(8,128)(2,1)} fusion(bf16[2,512,1280]{2,1,0:T(8,128)(2,1)S(1)} %collective-permute-done, bf16[2,512,1280]{2,1,0:T(8,128)(2,1)} %collective-permute-done.1, bf16[2,512,1280]{2,1,0:T(8,128)(2,1)} %collective-permute-done.2), kind=kLoop, calls=%fused_computation.45 | loop fusion | flops 23592960 | bytes 15728640 | tf_op jit(solution)/shard_map/concatenate | solution.py:43
  154.0 10.8 %all-to-all-done.3 = bf16[128,4,1280]{2,0,1:T(8,128)(2,1)} async-done(((bf16[128,4,1280]{2,0,1:T(8,128)(2,1)}), bf16[128,4,1280]{2,0,1:T(8,128)(2,1)}, u32[]{:S(2)}, u32[]{:S(2)}) %all-to-all-start.3) | async-done | bytes 1310752 | tf_op jit(solution)/shard_map/all_to_all | solution.py:31
  164.8 226.8 %while.19 = (s32[]{:T(128)}, bf16[10,512,128]{2,1,0:T(8,128)(2,1)}, bf16[10,512,128]{2,1,0:T(8,128)(2,1)}, bf16[10,512,128]{2,1,0:T(8,128)(2,1)}, bf16[10,512,12...) while((s32[]{:T(128)}, bf16[10,512,128]{2,1,0:T(8,128)(2,1)}, ...), condition=%wide.region_5.6_spmd.clone, body=%wide.region_0.5_spmd.clone.sunk | while | flops 1235941760 | bytes 64526704 | solution.py:112
  166.0 3.6 fusion.51
  211.4 3.6 fusion.51
  234.0 3.6 fusion.51
  302.0 3.6 fusion.51
  403.7 11.3 %all-to-all-done.4 = bf16[4,128,1280]{1,2,0:T(8,128)(2,1)S(1)} async-done(((bf16[4,128,1280]{1,2,0:T(8,128)(2,1)}), bf16[4,128,1280]{1,2,0:T(8,128)(2,1)S(1)}, u32[]{:S(2)}, u32[]{:S(2)}) %all-to-all-start.4) | async-done | bytes 1310752 | tf_op jit(solution)/shard_map/all_to_all | solution.py:119
  427.0 7.2 %all-to-all-done.5 = bf16[4,128,1280]{1,2,0:T(8,128)(2,1)S(1)} async-done(((bf16[4,128,1280]{1,2,0:T(8,128)(2,1)}), bf16[4,128,1280]{1,2,0:T(8,128)(2,1)S(1)}, u32[]{:S(2)}, u32[]{:S(2)}) %all-to-all-start.5) | async-done | bytes 1310752 | tf_op jit(solution)/shard_map/all_to_all | solution.py:120
  434.2 4.5 all-to-all-start.6
  447.3 5.9 all-to-all-done.6
  453.2 4.3 all-to-all-start.7
  457.5 130.3 %psum.7 = f32[10,128]{1,0:T(8,128)} all-reduce(f32[10,128]{1,0:T(8,128)S(1)} %get-tuple-element.85), channel_id=1, replica_groups=mesh['ctx'=64,'tsp'=4] {'ctx'}, use_global_device_ids=true, to_apply=%region_6.7 | all-reduce | flops 1280 | bytes 10240 | tf_op jit(solution)/shard_map/psum | solution.py:117
  (205 shorter events, 236.0 us)
Async XLA Ops:
  0.6 7.4 %copy-start.1 = (bf16[128,5120]{1,0:T(8,128)(2,1)S(1)}, bf16[128,5120]{1,0:T(8,128)(2,1)}, u32[]{:S(2)}) copy-start(bf16[128,5120]{1,0:T(8,128)(2,1)} %param.11) | copy-start | bytes 3932164
  3.2 20.3 %all-to-all-start.1 = ((bf16[128,4,1280]{2,0,1:T(8,128)(2,1)}), bf16[128,4,1280]{2,0,1:T(8,128)(2,1)}, u32[]{:S(2)}, u32[]{:S(2)}) async-start(bf16[128,4,1280]{2,0,1:T(8,128)(2,1)} %bitcast.80), calls=%async_computation.1 | async-start | bytes 2621440 | tf_op jit(solution)/shard_map/all_to_all | solution.py:29
  40.8 78.1 %copy-start.2 = (bf16[128,5120]{1,0:T(8,128)(2,1)S(1)}, bf16[128,5120]{1,0:T(8,128)(2,1)}, u32[]{:S(2)}) copy-start(bf16[128,5120]{1,0:T(8,128)(2,1)} %param.9) | copy-start | bytes 3932164
  42.8 38.6 %collective-permute-start = (bf16[2,512,1280]{2,1,0:T(8,128)(2,1)S(1)}, bf16[2,512,1280]{2,1,0:T(8,128)(2,1)S(1)}, u32[]{:S(2)}, u32[]{:S(2)}) collective-permute-start(bf16[2,512,1280]{2,1,0:T(8,128)(2,1)S(1)} %pad_maximum_fusion.7), channel_id=1, source_target_pairs={{0,4},{4,8},{8,12},{12,16},{16,20},{20,24},{24,28},{28,32},{32,36}... | collective-permute-start | bytes 7864328 | tf_op jit(solution)/shard_map/ppermute | solution.py:14
  81.4 33.0 %collective-permute-start.1 = (bf16[2,512,1280]{2,1,0:T(8,128)(2,1)S(1)}, bf16[2,512,1280]{2,1,0:T(8,128)(2,1)}, u32[]{:S(2)}, u32[]{:S(2)}) collective-permute-start(bf16[2,512,1280]{2,1,0:T(8,128)(2,1)S(1)} %collective-permute-done), channel_id=1, source_target_pairs={{0,4},{4,8},{8,12},{12,16},{16,20},{20,24},{24,28},{28,32},{32,36}... | collective-permute-start | bytes 7864328 | tf_op jit(solution)/shard_map/ppermute | solution.py:14
  114.4 33.4 %collective-permute-start.2 = (bf16[2,512,1280]{2,1,0:T(8,128)(2,1)}, bf16[2,512,1280]{2,1,0:T(8,128)(2,1)}, u32[]{:S(2)}, u32[]{:S(2)}) collective-permute-start(bf16[2,512,1280]{2,1,0:T(8,128)(2,1)} %collective-permute-done.1), channel_id=1, source_target_pairs={{0,4},{4,8},{8,12},{12,16},{16,20},{20,24},{24,28},{28,32},{32,36}... | collective-permute-start | bytes 7864328 | tf_op jit(solution)/shard_map/ppermute | solution.py:14
  120.1 22.7 %all-to-all-start = ((bf16[128,4,1280]{2,0,1:T(8,128)(2,1)}), bf16[128,4,1280]{2,0,1:T(8,128)(2,1)}, u32[]{:S(2)}, u32[]{:S(2)}) async-start(bf16[128,4,1280]{2,0,1:T(8,128)(2,1)} %bitcast.81), calls=%async_computation | async-start | bytes 2621440 | tf_op jit(solution)/shard_map/all_to_all | solution.py:28
  142.8 22.0 %all-to-all-start.3 = ((bf16[128,4,1280]{2,0,1:T(8,128)(2,1)}), bf16[128,4,1280]{2,0,1:T(8,128)(2,1)}, u32[]{:S(2)}, u32[]{:S(2)}) async-start(bf16[128,4,1280]{2,0,1:T(8,128)(2,1)} %bitcast.78), calls=%async_computation.3 | async-start | bytes 2621440 | tf_op jit(solution)/shard_map/all_to_all | solution.py:31
  180.6 1.5 copy-start
  203.2 1.4 copy-start
  225.9 1.4 copy-start
  248.5 1.4 copy-start
  271.2 1.4 copy-start
  293.9 1.4 copy-start
  316.5 1.4 copy-start
  339.2 1.5 copy-start
  361.9 1.5 copy-start
  384.6 1.5 copy-start
  394.7 20.2 %all-to-all-start.4 = ((bf16[4,128,1280]{1,2,0:T(8,128)(2,1)}), bf16[4,128,1280]{1,2,0:T(8,128)(2,1)S(1)}, u32[]{:S(2)}, u32[]{:S(2)}) async-start(bf16[4,128,1280]{1,2,0:T(8,128)(2,1)} %copy.45), calls=%async_computation.4 | async-start | bytes 2621440 | tf_op jit(solution)/shard_map/all_to_all | solution.py:119
  414.9 19.3 %all-to-all-start.5 = ((bf16[4,128,1280]{1,2,0:T(8,128)(2,1)}), bf16[4,128,1280]{1,2,0:T(8,128)(2,1)S(1)}, u32[]{:S(2)}, u32[]{:S(2)}) async-start(bf16[4,128,1280]{1,2,0:T(8,128)(2,1)} %copy.47), calls=%async_computation.5 | async-start | bytes 2621440 | tf_op jit(solution)/shard_map/all_to_all | solution.py:120
  434.2 18.9 %all-to-all-start.6 = ((bf16[4,128,1280]{1,2,0:T(8,128)(2,1)}), bf16[4,128,1280]{1,2,0:T(8,128)(2,1)}, u32[]{:S(2)}, u32[]{:S(2)}) async-start(bf16[4,128,1280]{1,2,0:T(8,128)(2,1)} %copy.49), calls=%async_computation.6 | async-start | bytes 2621440 | tf_op jit(solution)/shard_map/all_to_all | solution.py:121
  453.2 139.9 %all-to-all-start.7 = ((bf16[4,128,1280]{1,2,0:T(8,128)(2,1)}), bf16[4,128,1280]{1,2,0:T(8,128)(2,1)}, u32[]{:S(2)}, u32[]{:S(2)}) async-start(bf16[4,128,1280]{1,2,0:T(8,128)(2,1)} %copy.51), calls=%async_computation.7 | async-start | bytes 2621440 | tf_op jit(solution)/shard_map/all_to_all | solution.py:122
where the time goes:
time: 598 us; the launch traced here: 595 us
  blocking collectives  148 us (25%)
  waiting for transfers between devices  123 us (21%)
  matrix products  118 us (20%)
  local copies, waits for them, and re-layouts  99.6 us (17%)
  starting transfers between devices  48.2 us (8%)
  other arithmetic  31.5 us (5%)
  loops' own time  25.9 us (4%)
    psum x1, blocking collectives, shards(): grad_bias = lax.psum(results[4], 'ctx')  130 us
    ppermute x3, waiting for transfers between devices, passed_along(): lax.ppermute(value, axis, [(source, source + steps) for source in range(i...  57.9 us
    slice x10, local copies, waits for them, and re-layouts, one_head(): window[1]  36 us
    dot_general x10, matrix products, one_head(): lax.dot_general(shifted, key_rows, contract_cols, preferred_element_type=...  29.1 us
    another operation x1, loops' own time, shards(): results = lax.map(one_head, jnp.arange(local_heads, dtype=jnp.int32))  25.9 us
    dot_general x10, matrix products, one_head(): lax.dot_general(grad_scores[:, MEM:], shifted, contract_rows, preferred_e...  20.8 us
    dot_general x10, matrix products, one_head(): lax.dot_general(grad_rows, value_rows, contract_cols, preferred_element_t...  20.7 us
    dot_general x10, matrix products, one_head(): lax.dot_general(probs_half[:, MEM:], grad_rows, contract_rows, preferred_...  19.1 us
  transfers between devices with their start and end apart: 10, of which 9 were waited for; matrix products, arithmetic and copies ran while one was open for 5% of the time, Pallas kernels for 0%

commit v1 on v0

v1 whole, which is shorter than its diff:
```python
import functools
import math

import jax
import jax.numpy as jnp
from jax import lax
from jax.experimental import pallas as pl
from jax.experimental.pallas import tpu as pltpu
from jax.sharding import PartitionSpec as P

MESH = pl.DeviceIdType.MESH
MEM = 1536
ROWS = 512
PART = 128
HEAD = 128
TSP = 4
RING = 4
LOCAL = 5
SPAN = MEM + 2 * ROWS
WIDE = MEM + ROWS
HALF = 256
MASKED = -1e30
SCALING = 1.0 / math.sqrt(HEAD)
LOG2_SCALING = SCALING * math.log2(math.e)
LAST = (((1,), (1,)), ((), ()))
FIRST = (((0,), (0,)), ((), ()))


def kernel(
    depth,
    q_ref, k_ref, v_ref, g_ref, bias_ref, length_ref, end_ref,
    o_ref, gq_ref, gk_ref, gv_ref, gb_ref,
    q_buf, g_buf, k_buf, v_buf, o_buf, gq_buf, gk_buf, gv_buf,
    info, mask, part_bias, z_bias, y_bias, sum_bias,
    in_send, in_recv, mem_send, mem_recv, out_send, out_recv, info_sem, z_sem, y_sem,
):
    c, t = lax.axis_index("ctx"), lax.axis_index("tsp")
    shards = depth * RING * 2
    core = lax.rem(c, 2)
    pair = c // 2
    y = lax.rem(pair, RING)
    z = pair // RING

    def far(value, n):
        return lax.rem(value, n)

    def x_peer(dk, dt):
        return (pair * 2 + (core if dk == 0 else 1 - core), far(t + dt, TSP))

    def z_peer(dz):
        return ((far(z + dz, depth) * RING + y) * 2 + core, t)

    def y_peer(dk, dy):
        return ((z * RING + far(y + dy, RING)) * 2 + (core if dk == 0 else 1 - core), t)

    def ctx_peer(step):
        return (far(c + step + shards, shards), t)

    x_peers = [(dk, dt) for dt in (1, 2, 3) for dk in (0, 1)] + [(1, 0)]
    y_peers = [(dk, dy) for dy in (1, 2, 3) for dk in (0, 1)] + [(1, 0)]

    barrier = pltpu.get_barrier_semaphore()

    def greet(device):
        pl.semaphore_signal(barrier, inc=1, device_id=device, device_id_type=MESH)

    for dk, dt in x_peers:
        greet(x_peer(dk, dt))
    for dz in range(1, depth):
        greet(z_peer(dz))
    for dk, dy in y_peers:
        greet(y_peer(dk, dy))
    greet(ctx_peer(-2))
    greet(ctx_peer(-4))
    pl.semaphore_wait(barrier, 7 + depth - 1 + 7 + 2)

    sources = (k_ref, v_ref, q_ref, g_ref)
    own_rows = pl.ds(pl.multiple_of(t * PART, PART), PART)

    def landing(which, head, shard, rows):
        if which < 2:
            first = MEM + shard * ROWS
            buf = (k_buf, v_buf)[which]
        else:
            first = shard * ROWS
            buf = (q_buf, g_buf)[which - 2]
        return buf.at[head, pl.ds(pl.multiple_of(first + rows, PART), PART)]

    def scatter_in(arrays, head):
        for dk, dt in x_peers + [(0, 0)]:
            device = x_peer(dk, dt)
            to_core = core if dk == 0 else 1 - core
            column = (device[1] * 2 + to_core) * LOCAL + head
            columns = pl.ds(pl.multiple_of(column * HEAD, HEAD), HEAD)
            for which in arrays:
                source = sources[which].at[:, columns]
                target = landing(which, head, core, t * PART)
                if (dk, dt) == (0, 0):
                    pltpu.make_async_copy(source, target, in_recv.at[which, head]).start()
                else:
                    pltpu.make_async_remote_copy(
                        source, target, in_send.at[which], in_recv.at[which, head],
                        device_id=device, device_id_type=MESH,
                    ).start()

    def wait_in(arrays, head):
        for which in arrays:
            if which < 2:
                ref = (k_buf, v_buf)[which].at[head, pl.ds(MEM, 2 * ROWS)]
            else:
                ref = (q_buf, g_buf)[which - 2].at[head]
            pltpu.make_async_copy(ref, ref, in_recv.at[which, head]).wait()

    def send_memory(head):
        for which, buf in enumerate((k_buf, v_buf)):
            pltpu.make_async_remote_copy(
                buf.at[head, pl.ds(MEM, 2 * ROWS)], buf.at[head, pl.ds(ROWS, 2 * ROWS)],
                mem_send.at[which], mem_recv.at[which, head],
                device_id=ctx_peer(2), device_id_type=MESH,
            ).start()
            pltpu.make_async_remote_copy(
                buf.at[head, pl.ds(MEM + ROWS, ROWS)], buf.at[head, pl.ds(0, ROWS)],
                mem_send.at[which], mem_recv.at[which, head],
                device_id=ctx_peer(4), device_id_type=MESH,
            ).start()

    def wait_memory(head):
        for which, buf in enumerate((k_buf, v_buf)):
            ref = buf.at[head, pl.ds(0, MEM)]
            pltpu.make_async_copy(ref, ref, mem_recv.at[which, head]).wait()

    def first_sends(head, carry):
        scatter_in((0, 1), head)
        return carry

    lax.fori_loop(0, 3, first_sends, 0)

    usable = jnp.minimum(length_ref[0], c * ROWS)
    tile_row = lax.broadcasted_iota(jnp.int32, (8, 128), 0)
    info[core] = jnp.where(tile_row == 0, usable, end_ref[0]).astype(jnp.float32)
    swap = pltpu.make_async_remote_copy(
        info.at[core], info.at[core], info_sem.at[0], info_sem.at[1],
        device_id=x_peer(1, 0), device_id_type=MESH,
    )
    swap.start()
    swap.wait()

    def build_mask(step, carry):
        shard, block = step // (WIDE // 128), lax.rem(step, WIDE // 128)
        limit = info[shard]
        allowed_memory = limit[0:1]
        boundary = limit[1:2]
        row = lax.broadcasted_iota(jnp.int32, (ROWS, 128), 0).astype(jnp.float32)
        col = (lax.broadcasted_iota(jnp.int32, (ROWS, 128), 1) + block * 128).astype(jnp.float32)
        offset = col - float(MEM)
        row_first = jnp.where(row < boundary, 1.0, 0.0)
        col_first = jnp.where(offset < boundary, 1.0, 0.0)
        memory_ok = jnp.where(offset >= 0.0 - allowed_memory, row_first, 0.0)
        local_ok = jnp.where((offset <= row) & (row_first == col_first), 1.0, 0.0)
        ok = jnp.where(offset < 0.0, memory_ok, local_ok)
        mask[shard, :, pl.ds(pl.multiple_of(block * 128, 128), 128)] = jnp.where(ok > 0.5, 0.0, MASKED)
        return carry

    lax.fori_loop(0, 2 * (WIDE // 128), build_mask, 0)

    def gather_step(head, carry):
        @pl.when(head < LOCAL - 3)
        def _():
            scatter_in((0, 1), head + 3)

        @pl.when(head >= LOCAL - 3)
        def _():
            scatter_in((2, 3), head - (LOCAL - 3))

        wait_in((0, 1), head)

        @pl.when(head < 2)
        def _():
            send_memory(head)

        return carry

    lax.fori_loop(0, LOCAL, gather_step, 0)

    def last_sends(head, carry):
        scatter_in((2, 3), head)
        return carry

    lax.fori_loop(3, LOCAL, last_sends, 0)

    outputs = ((o_buf, o_ref), (gq_buf, gq_ref), (gk_buf, gk_ref), (gv_buf, gv_ref))

    def attend(head, shard):
        bias = bias_ref[pl.ds(core * LOCAL + head, 1), :]
        key_first = pl.multiple_of(shard * ROWS, ROWS)
        bias_total = jnp.zeros((8, HEAD), jnp.float32)
        key_parts, value_parts = [], []
        for half in range(2):
            rows = pl.ds(half * HALF, HALF)
            in_rows = pl.ds(pl.multiple_of(shard * ROWS + half * HALF, HALF), HALF)
            span = MEM + HALF * (half + 1)
            shifted = (q_buf[head, in_rows, :].astype(jnp.float32) + bias).astype(jnp.bfloat16)
            grad_rows = g_buf[head, in_rows, :]
            key_rows = k_buf[head, pl.ds(key_first, span), :]
            value_rows = v_buf[head, pl.ds(key_first, span), :]
            scores = lax.dot_general(shifted, key_rows, LAST, preferred_element_type=jnp.float32)
            scores = scores * LOG2_SCALING + mask[shard, rows, 0:span]
            peak = jnp.max(scores, axis=1, keepdims=True)
            weights = jnp.exp2(scores - peak)
            inverse = 1.0 / jnp.sum(weights, axis=1, keepdims=True)
            probs = weights * inverse
            probs_half = probs.astype(jnp.bfloat16)
            attended = jnp.dot(probs_half, value_rows, preferred_element_type=jnp.float32)
            grad_probs = lax.dot_general(grad_rows, value_rows, LAST, preferred_element_type=jnp.float32)
            centre = jnp.sum(probs * grad_probs, axis=1, keepdims=True)
            grad_scores = (probs * (grad_probs - centre) * SCALING).astype(jnp.bfloat16)
            grad_query = jnp.dot(grad_scores, key_rows, preferred_element_type=jnp.float32)
            out_rows = in_rows
            o_buf[head, out_rows, :] = attended.astype(jnp.bfloat16)
            gq_buf[head, out_rows, :] = grad_query.astype(jnp.bfloat16)
            bias_total += jnp.sum(grad_query.reshape(HALF // 8, 8, HEAD), axis=0)
            key_parts.append(
                lax.dot_general(grad_scores[:, MEM:], shifted, FIRST, preferred_element_type=jnp.float32)
            )
            value_parts.append(
                lax.dot_general(probs_half[:, MEM:], grad_rows, FIRST, preferred_element_type=jnp.float32)
            )
        for buf, parts in ((gk_buf, key_parts), (gv_buf, value_parts)):
            low = pl.ds(pl.multiple_of(shard * ROWS, HALF), HALF)
            high = pl.ds(pl.multiple_of(shard * ROWS + HALF, HALF), HALF)
            buf[head, low, :] = (parts[0] + parts[1][:HALF]).astype(jnp.bfloat16)
            buf[head, high, :] = parts[1][HALF:].astype(jnp.bfloat16)
        return bias_total

    def send_out(head, shard, dt, local):
        to_part = far(t + dt, TSP)
        column = (t * 2 + core) * LOCAL + head
        columns = pl.ds(pl.multiple_of(column * HEAD, HEAD), HEAD)
        rows = pl.ds(pl.multiple_of(shard * ROWS + to_part * PART, PART), PART)
        for which, (buf, ref) in enumerate(outputs):
            source, target = buf.at[head, rows], ref.at[:, columns]
            if local:
                pltpu.make_async_copy(source, target, out_recv.at[which]).start()
            else:
                pltpu.make_async_remote_copy(
                    source, target, out_send.at[which], out_recv.at[which],
                    device_id=(pair * 2 + shard, to_part), device_id_type=MESH,
                ).start()

    def head_step(head, carry):
        wait_memory(head)

        @pl.when(head < LOCAL - 2)
        def _():
            send_memory(head + 2)

        wait_in((2, 3), head)

        def shard_step(i, total):
            shard = far(core + 1 + i, 2)
            total = total + attend(head, shard)
            for dt in (2, 1, 3):
                send_out(head, shard, dt, False)

            @pl.when(i == 0)
            def _():
                send_out(head, shard, 0, False)

            @pl.when(i == 1)
            def _():
                send_out(head, shard, 0, True)

            return total

        part_bias[head] = lax.fori_loop(0, 2, shard_step, jnp.zeros((8, HEAD), jnp.float32))
        return carry

    lax.fori_loop(0, LOCAL, head_step, 0)

    z_bias[z] = part_bias[...]
    for dz in range(1, depth):
        pltpu.make_async_remote_copy(
            part_bias, z_bias.at[z], z_sem.at[0], z_sem.at[1],
            device_id=z_peer(dz), device_id_type=MESH,
        ).start()
    others = z_bias.at[pl.ds(0, depth - 1)]
    pltpu.make_async_copy(others, others, z_sem.at[1]).wait()
    sum_bias[...] = jnp.sum(z_bias[...], axis=0)
    y_bias[core, y] = sum_bias[...]
    for dk, dy in y_peers:
        pltpu.make_async_remote_copy(
            sum_bias, y_bias.at[core, y], y_sem.at[0], y_sem.at[1],
            device_id=y_peer(dk, dy), device_id_type=MESH,
        ).start()
    others_y = z_bias.at[pl.ds(0, 7)]
    pltpu.make_async_copy(others_y, others_y, y_sem.at[1]).wait()
    for which in range(2):
        total = jnp.sum(jnp.sum(y_bias[which], axis=0), axis=1)
        gb_ref[pl.ds(which * LOCAL, LOCAL), :] = total

    for which in range(4):
        ref = outputs[which][1]
        pltpu.make_async_copy(ref, ref, out_recv.at[which]).wait()
        part = ref.at[:, pl.ds(0, 7 * LOCAL * HEAD)]
        pltpu.make_async_copy(part, part, out_send.at[which]).wait()
        pltpu.make_async_copy(part, part, in_send.at[which]).wait()
    for which, buf in enumerate((k_buf, v_buf)):
        ref = buf.at[:, pl.ds(0, MEM)]
        pltpu.make_async_copy(ref, ref, mem_send.at[which]).wait()
    pltpu.make_async_copy(others, others, z_sem.at[0]).wait()
    pltpu.make_async_copy(others_y, others_y, y_sem.at[0]).wait()


def solution(mesh):
    depth = mesh.shape["ctx"] // (2 * RING)
    half = jnp.bfloat16

    def step(queries, keys, values, cotangent, content_bias, memory_lengths, segment_ends):
        any_spec = pl.BlockSpec(memory_space=pl.ANY)
        vmem_spec = pl.BlockSpec(memory_space=pltpu.VMEM)
        smem_spec = pl.BlockSpec(memory_space=pltpu.SMEM)
        slab = jax.ShapeDtypeStruct(queries.shape, half)
        dma, vmem = pltpu.SemaphoreType.DMA, pltpu.VMEM
        return pl.pallas_call(
            functools.partial(kernel, depth),
            out_shape=(slab, slab, slab, slab, jax.ShapeDtypeStruct(content_bias.shape, jnp.float32)),
            in_specs=[any_spec] * 4 + [vmem_spec, smem_spec, smem_spec],
            out_specs=[any_spec] * 4 + [vmem_spec],
            scratch_shapes=[
                vmem((LOCAL, 2 * ROWS, HEAD), half),
                vmem((LOCAL, 2 * ROWS, HEAD), half),
                vmem((LOCAL, SPAN, HEAD), half),
                vmem((LOCAL, SPAN, HEAD), half),
                vmem((LOCAL, 2 * ROWS, HEAD), half),
                vmem((LOCAL, 2 * ROWS, HEAD), half),
                vmem((LOCAL, 2 * ROWS, HEAD), half),
                vmem((LOCAL, 2 * ROWS, HEAD), half),
                vmem((2, 8, 128), jnp.float32),
                vmem((2, ROWS, WIDE), jnp.float32),
                vmem((LOCAL, 8, HEAD), jnp.float32),
                vmem((depth, LOCAL, 8, HEAD), jnp.float32),
                vmem((2, RING, LOCAL, 8, HEAD), jnp.float32),
                vmem((LOCAL, 8, HEAD), jnp.float32),
                dma((4,)),
                dma((4, LOCAL)),
                dma((2,)),
                dma((2, LOCAL)),
                dma((4,)),
                dma((4,)),
                dma((2,)),
                dma((2,)),
                dma((2,)),
            ],
            compiler_params=pltpu.CompilerParams(
                collective_id=1, has_side_effects=True, vmem_limit_bytes=60 * 1024 * 1024
            ),
            cost_estimate=pl.CostEstimate(flops=12 * 10**9, bytes_accessed=20 * 10**6, transcendentals=10**7),
        )(queries, keys, values, cotangent, content_bias, memory_lengths, segment_ends)

    tokens = P(("ctx", "tsp"), None)
    return jax.shard_map(
        step,
        mesh=mesh,
        in_specs=(tokens, tokens, tokens, tokens, P("tsp", None), P("ctx"), P("ctx")),
        out_specs=(tokens, tokens, tokens, tokens, P("tsp", None)),
        check_vma=False,
    )
```

time: 598 us -> 156 us (0.26)
  blocking collectives: 148 us -> 0 us
  Pallas kernels: 0 us -> 146 us
  waiting for transfers between devices: 123 us -> 0 us
  matrix products: 118 us -> 0 us
  local copies, waits for them, and re-layouts: 99.6 us -> 7.8 us
  starting transfers between devices: 48.2 us -> 0 us
  other arithmetic: 31.5 us -> 0 us
  loops' own time: 25.9 us -> 0 us
    pallas_call x0 -> x1, Pallas kernels: none -> 146 us  [step(): pl.pallas_call(functools.partial(kernel, depth), out_shape=(slab, slab, s...]
    psum x1 -> x0, blocking collectives: 130 us -> none  [shards(): grad_bias = lax.psum(results[4], 'ctx')]
    dot_general x60 -> x0, matrix products: 118 us -> none  [the longest x10 29.1 us: one_head(): lax.dot_general(shifted, key_rows, contract_cols, preferred_element_type=...]
    all_to_all x7 -> x0, waiting for transfers between devices: 65.1 us -> none  [the longest x1 15.4 us: shards(): lax.all_to_all(keys, 'tsp', split_axis=1, concat_axis=0, tiled=True)]
    ppermute x3 -> x0, waiting for transfers between devices: 57.9 us -> none  [passed_along(): lax.ppermute(value, axis, [(source, source + steps) for source in range(i...]
    slice x10 -> x0, local copies, waits for them, and re-layouts: 36 us -> none  [one_head(): window[1]]
    all_to_all x7 -> x0, starting transfers between devices: 29.3 us -> none  [the longest x1 4.84 us: shards(): lax.all_to_all(keys, 'tsp', split_axis=1, concat_axis=0, tiled=True)]
    another operation x1 -> x0, loops' own time: 25.9 us -> none  [shards(): results = lax.map(one_head, jnp.arange(local_heads, dtype=jnp.int32))]
  transfers between devices with their start and end apart: 10 -> 0, of which waited for: 9 -> 0; matrix products, arithmetic and copies ran while one was open for 5% -> 0% of each run, Pallas kernels for 0% -> 0%
where the time goes in v1:
time: 156 us
  Pallas kernels  146 us (94%)
  local copies, waits for them, and re-layouts  7.8 us (5%)
  between operations  1.95 us (1%)
    pallas_call x1, Pallas kernels, step(): pl.pallas_call(functools.partial(kernel, depth), out_shape=(slab, slab, s...  146 us
    unnamed x13, local copies, waits for them, and re-layouts  7.8 us

profile of v1, /device:TPU:1, one launch (start us, length us, event | category | flops | bytes accessed | tf_op | source)
XLA Modules:
  0.0 155.7 jit_solution(2906037687442702745)
XLA Ops:
  1.9 146.0 %shard_map.110 = (bf16[128,5120]{1,0:T(8,128)(2,1)}, bf16[128,5120]{1,0:T(8,128)(2,1)}, bf16[128,5120]{1,0:T(8,128)(2,1)}, bf16[128,5120]{1,0:T(8,128)(2,1)}, f32[10,128]{1,0:T(8,128)}) custom-call(bf16[128,5120]{1,0:T(8,128)(2,1)} %q_ref.1, bf16[128,5120]{1,0:T(8,128)(2,1)} %k_ref.1, bf16[128,5120]{1,0:T(8,128)(2,1)} %v_ref.1, bf16[128,5120]{1,0:T(8,128)(2,1)} %g_ref.1, ...), custom_call_target="tpu_custom_call" | custom-call | flops 12000000000 | bytes 20000000 | tf_op jit(solution)/shard_map/pallas_call | solution.py:324
  147.9 0.0 copy-start.2
  147.9 2.6 %copy.19 = bf16[128,5120]{1,0:T(8,128)(2,1)} copy(bf16[128,5120]{1,0:T(8,128)(2,1)} %get-tuple-element.10) | data formatting | bytes 2621440
  150.5 0.0 copy-done.2
  150.5 0.0 copy-start.1
  150.5 1.1 copy.20
  151.5 0.7 copy-done.1
  152.3 0.0 copy-start
  152.3 1.1 copy.21
  153.3 0.7 copy-done
  154.0 0.0 copy-start.3
  154.1 1.1 copy.22
  155.1 0.0 copy-done.3
  155.1 0.6 copy.23
Async XLA Ops:
  147.9 2.6 %copy-start.2 = (bf16[128,5120]{1,0:T(8,128)(2,1)S(1)}, bf16[128,5120]{1,0:T(8,128)(2,1)}, u32[]{:S(2)}) copy-start(bf16[128,5120]{1,0:T(8,128)(2,1)} %get-tuple-element.11) | copy-start | bytes 3932164
  150.5 1.8 %copy-start.1 = (bf16[128,5120]{1,0:T(8,128)(2,1)S(1)}, bf16[128,5120]{1,0:T(8,128)(2,1)}, u32[]{:S(2)}) copy-start(bf16[128,5120]{1,0:T(8,128)(2,1)} %get-tuple-element.12) | copy-start | bytes 3932164
  152.3 1.8 %copy-start = (bf16[128,5120]{1,0:T(8,128)(2,1)S(1)}, bf16[128,5120]{1,0:T(8,128)(2,1)}, u32[]{:S(2)}) copy-start(bf16[128,5120]{1,0:T(8,128)(2,1)} %get-tuple-element.13) | copy-start | bytes 3932164
  154.0 1.1 copy-start.3

commit v2 on v1

--- a/solution.py
+++ b/solution.py
@@ -19,6 +19,8 @@
 SPAN = MEM + 2 * ROWS
 WIDE = MEM + ROWS
 HALF = 256
+AHEAD = 2
+VLIMIT = 48
 MASKED = -1e30
 SCALING = 1.0 / math.sqrt(HEAD)
 LOG2_SCALING = SCALING * math.log2(math.e)
@@ -31,8 +33,8 @@
     q_ref, k_ref, v_ref, g_ref, bias_ref, length_ref, end_ref,
     o_ref, gq_ref, gk_ref, gv_ref, gb_ref,
     q_buf, g_buf, k_buf, v_buf, o_buf, gq_buf, gk_buf, gv_buf,
-    info, mask, part_bias, z_bias, y_bias, sum_bias,
-    in_send, in_recv, mem_send, mem_recv, out_send, out_recv, info_sem, z_sem, y_sem,
+    k_relay, v_relay, info, mask, part_bias, z_bias, y_bias, sum_bias,
+    in_send, in_recv, mem_send, mem_recv, relay_send, relay_recv, out_send, out_recv, info_sem, z_sem, y_sem,
 ):
     c, t = lax.axis_index("ctx"), lax.axis_index("tsp")
     shards = depth * RING * 2
@@ -56,6 +58,14 @@
     def ctx_peer(step):
         return (far(c + step + shards, shards), t)
 
+    def place(z_at, y_at):
+        return ((far(z_at + depth, depth) * RING + far(y_at + RING, RING)) * 2 + core, t)
+
+    relay_to = place(z, y - 1)
+    relay_from = place(z, y + 1)
+    onward_to = place(z + jnp.where((y == 1) | (y == 2), 1, 0), y - 1)
+    onward_from = place(z - jnp.where((y == 0) | (y == 1), 1, 0), y + 1)
+
     x_peers = [(dk, dt) for dt in (1, 2, 3) for dk in (0, 1)] + [(1, 0)]
     y_peers = [(dk, dy) for dy in (1, 2, 3) for dk in (0, 1)] + [(1, 0)]
 
@@ -71,8 +81,9 @@
     for dk, dy in y_peers:
         greet(y_peer(dk, dy))
     greet(ctx_peer(-2))
-    greet(ctx_peer(-4))
-    pl.semaphore_wait(barrier, 7 + depth - 1 + 7 + 2)
+    greet(relay_from)
+    greet(onward_from)
+    pl.semaphore_wait(barrier, 7 + depth - 1 + 7 + 3)
 
     sources = (k_ref, v_ref, q_ref, g_ref)
     own_rows = pl.ds(pl.multiple_of(t * PART, PART), PART)
@@ -119,9 +130,18 @@
                 device_id=ctx_peer(2), device_id_type=MESH,
             ).start()
             pltpu.make_async_remote_copy(
-                buf.at[head, pl.ds(MEM + ROWS, ROWS)], buf.at[head, pl.ds(0, ROWS)],
+                buf.at[head, pl.ds(MEM + ROWS, ROWS)], (k_relay, v_relay)[which].at[head],
+                relay_send.at[which], relay_recv.at[which, head],
+                device_id=relay_to, device_id_type=MESH,
+            ).start()
+
+    def forward(head):
+        for which, (relay, buf) in enumerate(((k_relay, k_buf), (v_relay, v_buf))):
+            pltpu.make_async_copy(relay.at[head], relay.at[head], relay_recv.at[which, head]).wait()
+            pltpu.make_async_remote_copy(
+                relay.at[head], buf.at[head, pl.ds(0, ROWS)],
                 mem_send.at[which], mem_recv.at[which, head],
-                device_id=ctx_peer(4), device_id_type=MESH,
+                device_id=onward_to, device_id_type=MESH,
             ).start()
 
     def wait_memory(head):
@@ -133,7 +153,7 @@
         scatter_in((0, 1), head)
         return carry
 
-    lax.fori_loop(0, 3, first_sends, 0)
+    lax.fori_loop(0, AHEAD, first_sends, 0)
 
     usable = jnp.minimum(length_ref[0], c * ROWS)
     tile_row = lax.broadcasted_iota(jnp.int32, (8, 128), 0)
@@ -164,19 +184,23 @@
     lax.fori_loop(0, 2 * (WIDE // 128), build_mask, 0)
 
     def gather_step(head, carry):
-        @pl.when(head < LOCAL - 3)
-        def _():
-            scatter_in((0, 1), head + 3)
-
-        @pl.when(head >= LOCAL - 3)
-        def _():
-            scatter_in((2, 3), head - (LOCAL - 3))
-
         wait_in((0, 1), head)
 
         @pl.when(head < 2)
         def _():
             send_memory(head)
+
+        @pl.when(head < LOCAL - AHEAD)
+        def _():
+            scatter_in((0, 1), head + AHEAD)
+
+        @pl.when(head >= LOCAL - AHEAD)
+        def _():
+            scatter_in((2, 3), head - (LOCAL - AHEAD))
+
+        @pl.when((head >= 2) & (head < 4))
+        def _():
+            forward(head - 2)
 
         return carry
 
@@ -186,7 +210,7 @@
         scatter_in((2, 3), head)
         return carry
 
-    lax.fori_loop(3, LOCAL, last_sends, 0)
+    lax.fori_loop(AHEAD, LOCAL, last_sends, 0)
 
     outputs = ((o_buf, o_ref), (gq_buf, gq_ref), (gk_buf, gk_ref), (gv_buf, gv_ref))
 
@@ -273,6 +297,11 @@
             return total
 
         part_bias[head] = lax.fori_loop(0, 2, shard_step, jnp.zeros((8, HEAD), jnp.float32))
+
+        @pl.when(head < LOCAL - 2)
+        def _():
+            forward(head + 2)
+
         return carry
 
     lax.fori_loop(0, LOCAL, head_step, 0)
@@ -307,8 +336,19 @@
     for which, buf in enumerate((k_buf, v_buf)):
         ref = buf.at[:, pl.ds(0, MEM)]
         pltpu.make_async_copy(ref, ref, mem_send.at[which]).wait()
+        relay = (k_relay, v_relay)[which]
+        pltpu.make_async_copy(relay, relay, relay_send.at[which]).wait()
     pltpu.make_async_copy(others, others, z_sem.at[0]).wait()
     pltpu.make_async_copy(others_y, others_y, y_sem.at[0]).wait()
+
+
+def write_out(o_in, gq_in, gk_in, gv_in, gb_in, o_ref, gq_ref, gk_ref, gv_ref, gb_ref, sem):
+    pairs = ((o_in, o_ref), (gq_in, gq_ref), (gk_in, gk_ref), (gv_in, gv_ref), (gb_in, gb_ref))
+    copies = [pltpu.make_async_copy(source, target, sem.at[i]) for i, (source, target) in enumerate(pairs)]
+    for copy in copies:
+        copy.start()
+    for copy in copies:
+        copy.wait()
 
 
 def solution(mesh):
@@ -321,7 +361,7 @@
         smem_spec = pl.BlockSpec(memory_space=pltpu.SMEM)
         slab = jax.ShapeDtypeStruct(queries.shape, half)
         dma, vmem = pltpu.SemaphoreType.DMA, pltpu.VMEM
-        return pl.pallas_call(
+        found = pl.pallas_call(
             functools.partial(kernel, depth),
             out_shape=(slab, slab, slab, slab, jax.ShapeDtypeStruct(content_bias.shape, jnp.float32)),
             in_specs=[any_spec] * 4 + [vmem_spec, smem_spec, smem_spec],
@@ -335,6 +375,8 @@
                 vmem((LOCAL, 2 * ROWS, HEAD), half),
                 vmem((LOCAL, 2 * ROWS, HEAD), half),
                 vmem((LOCAL, 2 * ROWS, HEAD), half),
+                vmem((LOCAL, ROWS, HEAD), half),
+                vmem((LOCAL, ROWS, HEAD), half),
                 vmem((2, 8, 128), jnp.float32),
                 vmem((2, ROWS, WIDE), jnp.float32),
                 vmem((LOCAL, 8, HEAD), jnp.float32),
@@ -345,6 +387,8 @@
                 dma((4, LOCAL)),
                 dma((2,)),
                 dma((2, LOCAL)),
+                dma((2,)),
+                dma((2, LOCAL)),
                 dma((4,)),
                 dma((4,)),
                 dma((2,)),
@@ -352,10 +396,18 @@
                 dma((2,)),
             ],
             compiler_params=pltpu.CompilerParams(
-                collective_id=1, has_side_effects=True, vmem_limit_bytes=60 * 1024 * 1024
+                collective_id=1, has_side_effects=True, vmem_limit_bytes=VLIMIT * 1024 * 1024
             ),
             cost_estimate=pl.CostEstimate(flops=12 * 10**9, bytes_accessed=20 * 10**6, transcendentals=10**7),
         )(queries, keys, values, cotangent, content_bias, memory_lengths, segment_ends)
+        return pl.pallas_call(
+            write_out,
+            out_shape=(slab, slab, slab, slab, jax.ShapeDtypeStruct(content_bias.shape, jnp.float32)),
+            in_specs=[any_spec] * 5,
+            out_specs=[any_spec] * 5,
+            scratch_shapes=[dma((5,))],
+            compiler_params=pltpu.CompilerParams(vmem_limit_bytes=16 * 1024 * 1024),
+        )(*found)
 
     tokens = P(("ctx", "tsp"), None)
     return jax.shard_map(

time: 156 us -> 129 us (0.83)
  Pallas kernels: 146 us -> 127 us
  local copies, waits for them, and re-layouts: 7.8 us -> 0.69 us
    pallas_call x1, Pallas kernels: 146 us -> 124 us  [step(): pl.pallas_call(functools.partial(kernel, depth), out_shape=(slab, slab, s...]
    unnamed x13 -> x2, local copies, waits for them, and re-layouts: 7.8 us -> 0.69 us
    pallas_call x0 -> x1, Pallas kernels: none -> 2.4 us  [step(): pl.pallas_call(write_out, out_shape=(slab, slab, slab, slab, jax.ShapeDty...]
where the time goes in v2:
time: 129 us
  Pallas kernels  127 us (98%)
  between operations  1.94 us (2%)
    pallas_call x1, Pallas kernels, step(): pl.pallas_call(functools.partial(kernel, depth), out_shape=(slab, slab, s...  124 us

profile of v2, /device:TPU:1, one launch (start us, length us, event | category | flops | bytes accessed | tf_op | source)
XLA Modules:
  0.0 129.3 jit_solution(12896256243238169344)
XLA Ops:
  1.9 0.0 copy-start
  1.9 0.7 copy-done
  2.6 124.3 %shard_map.110 = (bf16[128,5120]{1,0:T(8,128)(2,1)S(1)}, bf16[128,5120]{1,0:T(8,128)(2,1)S(1)}, bf16[128,5120]{1,0:T(8,128)(2,1)S(1)}, bf16[128,5120]{1,0:T(8,128)(2,1)S(1)}, f32[10,128]{1,0:T(8,128)S(1)}) custom-call(bf16[128,5120]{1,0:T(8,128)(2,1)} %q_ref.1, bf16[128,5120]{1,0:T(8,128)(2,1)} %k_ref.1, bf16[128,5120]{1,0:T(8,128)(2,1)} %v_ref.1, ...), custom_call_target="tpu_custom_call" | custom-call | flops 12000000000 | bytes 20000000 | tf_op jit(solution)/shard_map/pallas_call | solution.py:364
  126.9 2.4 %shard_map.111 = (bf16[128,5120]{1,0:T(8,128)(2,1)}, bf16[128,5120]{1,0:T(8,128)(2,1)}, bf16[128,5120]{1,0:T(8,128)(2,1)}, bf16[128,5120]{1,0:T(8,128)(2,1)}, f32[10,128]{1,0:T(8,128)}) custom-call(bf16[128,5120]{1,0:T(8,128)(2,1)S(1)} %get-tuple-element.10.o_in, bf16[128,5120]{1,0:T(8,128)(2,1)S(1)} %get-tuple-element.11.gq_in, ...), custom_call_target="tpu_custom_call" | custom-call | tf_op jit(solution)/shard_map/pallas_call | solution.py:403
Async XLA Ops:
  1.9 0.7 copy-start

commit v3 on v2

--- a/solution.py
+++ b/solution.py
@@ -34,7 +34,7 @@
     o_ref, gq_ref, gk_ref, gv_ref, gb_ref,
     q_buf, g_buf, k_buf, v_buf, o_buf, gq_buf, gk_buf, gv_buf,
     k_relay, v_relay, info, mask, part_bias, z_bias, y_bias, sum_bias,
-    in_send, in_recv, mem_send, mem_recv, relay_send, relay_recv, out_send, out_recv, info_sem, z_sem, y_sem,
+    in_send, in_recv, mem_send, mem_recv, relay_send, relay_recv, out_send, out_recv, info_sem, z_sem, z_recv, y_sem, y_recv, hello,
 ):
     c, t = lax.axis_index("ctx"), lax.axis_index("tsp")
     shards = depth * RING * 2
@@ -49,12 +49,6 @@
     def x_peer(dk, dt):
         return (pair * 2 + (core if dk == 0 else 1 - core), far(t + dt, TSP))
 
-    def z_peer(dz):
-        return ((far(z + dz, depth) * RING + y) * 2 + core, t)
-
-    def y_peer(dk, dy):
-        return ((z * RING + far(y + dy, RING)) * 2 + (core if dk == 0 else 1 - core), t)
-
     def ctx_peer(step):
         return (far(c + step + shards, shards), t)
 
@@ -67,7 +61,6 @@
     onward_from = place(z - jnp.where((y == 0) | (y == 1), 1, 0), y + 1)
 
     x_peers = [(dk, dt) for dt in (1, 2, 3) for dk in (0, 1)] + [(1, 0)]
-    y_peers = [(dk, dy) for dy in (1, 2, 3) for dk in (0, 1)] + [(1, 0)]
 
     barrier = pltpu.get_barrier_semaphore()
 
@@ -76,14 +69,12 @@
 
     for dk, dt in x_peers:
         greet(x_peer(dk, dt))
-    for dz in range(1, depth):
-        greet(z_peer(dz))
-    for dk, dy in y_peers:
-        greet(y_peer(dk, dy))
     greet(ctx_peer(-2))
     greet(relay_from)
     greet(onward_from)
-    pl.semaphore_wait(barrier, 7 + depth - 1 + 7 + 3)
+    greet(place(z - 1, y))
+    pl.semaphore_wait(barrier, 7 + 4)
+    pl.semaphore_signal(hello, inc=1, device_id=place(z + 1, y), device_id_type=MESH)
 
     sources = (k_ref, v_ref, q_ref, g_ref)
     own_rows = pl.ds(pl.multiple_of(t * PART, PART), PART)
@@ -148,6 +139,8 @@
         for which, buf in enumerate((k_buf, v_buf)):
             ref = buf.at[head, pl.ds(0, MEM)]
             pltpu.make_async_copy(ref, ref, mem_recv.at[which, head]).wait()
+
+    part_bias[...] = jnp.zeros_like(part_bias)
 
     def first_sends(head, carry):
         scatter_in((0, 1), head)
@@ -306,26 +299,34 @@
 
     lax.fori_loop(0, LOCAL, head_step, 0)
 
-    z_bias[z] = part_bias[...]
-    for dz in range(1, depth):
-        pltpu.make_async_remote_copy(
-            part_bias, z_bias.at[z], z_sem.at[0], z_sem.at[1],
-            device_id=z_peer(dz), device_id_type=MESH,
-        ).start()
-    others = z_bias.at[pl.ds(0, depth - 1)]
-    pltpu.make_async_copy(others, others, z_sem.at[1]).wait()
-    sum_bias[...] = jnp.sum(z_bias[...], axis=0)
-    y_bias[core, y] = sum_bias[...]
-    for dk, dy in y_peers:
-        pltpu.make_async_remote_copy(
-            sum_bias, y_bias.at[core, y], y_sem.at[0], y_sem.at[1],
-            device_id=y_peer(dk, dy), device_id_type=MESH,
-        ).start()
-    others_y = z_bias.at[pl.ds(0, 7)]
-    pltpu.make_async_copy(others_y, others_y, y_sem.at[1]).wait()
+    def gather_ring(parts, own, size, ups, up_to, down_to, sends, receives):
+        downs = size - 1 - ups
+        for step in range(max(ups, downs)):
+            incoming = []
+            for way, count, device in ((1, ups, up_to), (-1, downs, down_to)):
+                if step < count:
+                    outgoing = far(own - way * step + size, size)
+                    pltpu.make_async_remote_copy(
+                        parts.at[outgoing], parts.at[outgoing], sends, receives.at[outgoing],
+                        device_id=device, device_id_type=MESH,
+                    ).start()
+                    incoming.append(far(own - way * (step + 1) + size, size))
+            for slot in incoming:
+                pltpu.make_async_copy(parts.at[slot], parts.at[slot], receives.at[slot]).wait()
+        return jnp.sum(parts[...], axis=0)
+
+    z_bias[z] = jnp.sum(part_bias[...], axis=1)
+    pl.semaphore_wait(hello, 1)
+    y_bias[y] = gather_ring(z_bias, z, depth, depth // 2, place(z + 1, y), place(z - 1, y), z_sem, z_recv)
+    sum_bias[core] = gather_ring(y_bias, y, RING, 1, relay_from, relay_to, y_sem, y_recv)
+    swap_bias = pltpu.make_async_remote_copy(
+        sum_bias.at[core], sum_bias.at[core], info_sem.at[0], info_sem.at[1],
+        device_id=x_peer(1, 0), device_id_type=MESH,
+    )
+    swap_bias.start()
+    swap_bias.wait()
     for which in range(2):
-        total = jnp.sum(jnp.sum(y_bias[which], axis=0), axis=1)
-        gb_ref[pl.ds(which * LOCAL, LOCAL), :] = total
+        gb_ref[pl.ds(which * LOCAL, LOCAL), :] = sum_bias[which, 0:LOCAL]
 
     for which in range(4):
         ref = outputs[which][1]
@@ -338,8 +339,10 @@
         pltpu.make_async_copy(ref, ref, mem_send.at[which]).wait()
         relay = (k_relay, v_relay)[which]
         pltpu.make_async_copy(relay, relay, relay_send.at[which]).wait()
-    pltpu.make_async_copy(others, others, z_sem.at[0]).wait()
-    pltpu.make_async_copy(others_y, others_y, y_sem.at[0]).wait()
+    sent = z_bias.at[pl.ds(0, depth - 1)]
+    pltpu.make_async_copy(sent, sent, z_sem).wait()
+    sent = y_bias.at[pl.ds(0, RING - 1)]
+    pltpu.make_async_copy(sent, sent, y_sem).wait()
 
 
 def write_out(o_in, gq_in, gk_in, gv_in, gb_in, o_ref, gq_ref, gk_ref, gv_ref, gb_ref, sem):
@@ -379,10 +382,10 @@
                 vmem((LOCAL, ROWS, HEAD), half),
                 vmem((2, 8, 128), jnp.float32),
                 vmem((2, ROWS, WIDE), jnp.float32),
-                vmem((LOCAL, 8, HEAD), jnp.float32),
-                vmem((depth, LOCAL, 8, HEAD), jnp.float32),
-                vmem((2, RING, LOCAL, 8, HEAD), jnp.float32),
-                vmem((LOCAL, 8, HEAD), jnp.float32),
+                vmem((8, 8, HEAD), jnp.float32),
+                vmem((depth, 8, HEAD), jnp.float32),
+                vmem((RING, 8, HEAD), jnp.float32),
+                vmem((2, 8, HEAD), jnp.float32),
                 dma((4,)),
                 dma((4, LOCAL)),
                 dma((2,)),
@@ -392,8 +395,11 @@
                 dma((4,)),
                 dma((4,)),
                 dma((2,)),
-                dma((2,)),
-                dma((2,)),
+                dma(()),
+                dma((depth,)),
+                dma(()),
+                dma((RING,)),
+                pltpu.SemaphoreType.REGULAR,
             ],
             compiler_params=pltpu.CompilerParams(
                 collective_id=1, has_side_effects=True, vmem_limit_bytes=VLIMIT * 1024 * 1024

time: 129 us -> 126 us (0.977)
  Pallas kernels: 127 us -> 123 us
    pallas_call x1, Pallas kernels: 124 us -> 120 us  [step(): pl.pallas_call(functools.partial(kernel, depth), out_shape=(slab, slab, s...]
where the time goes in v3:
time: 126 us
  Pallas kernels  123 us (98%)
  between operations  1.94 us (2%)
    pallas_call x1, Pallas kernels, step(): pl.pallas_call(functools.partial(kernel, depth), out_shape=(slab, slab, s...  120 us

profile of v3, /device:TPU:1, one launch (start us, length us, event | category | flops | bytes accessed | tf_op | source)
XLA Modules:
  0.0 125.5 jit_solution(12433456551554500896)
XLA Ops:
  1.9 0.0 copy-start
  1.9 0.7 copy-done
  2.6 120.5 %shard_map.110 = (bf16[128,5120]{1,0:T(8,128)(2,1)S(1)}, bf16[128,5120]{1,0:T(8,128)(2,1)S(1)}, bf16[128,5120]{1,0:T(8,128)(2,1)S(1)}, bf16[128,5120]{1,0:T(8,128)(2,1)S(1)}, f32[10,128]{1,0:T(8,128)S(1)}) custom-call(bf16[128,5120]{1,0:T(8,128)(2,1)} %q_ref.1, bf16[128,5120]{1,0:T(8,128)(2,1)} %k_ref.1, bf16[128,5120]{1,0:T(8,128)(2,1)} %v_ref.1, ...), custom_call_target="tpu_custom_call" | custom-call | flops 12000000000 | bytes 20000000 | tf_op jit(solution)/shard_map/pallas_call | solution.py:367
  123.1 2.4 %shard_map.111 = (bf16[128,5120]{1,0:T(8,128)(2,1)}, bf16[128,5120]{1,0:T(8,128)(2,1)}, bf16[128,5120]{1,0:T(8,128)(2,1)}, bf16[128,5120]{1,0:T(8,128)(2,1)}, f32[10,128]{1,0:T(8,128)}) custom-call(bf16[128,5120]{1,0:T(8,128)(2,1)S(1)} %get-tuple-element.10.o_in, bf16[128,5120]{1,0:T(8,128)(2,1)S(1)} %get-tuple-element.11.gq_in, ...), custom_call_target="tpu_custom_call" | custom-call | tf_op jit(solution)/shard_map/pallas_call | solution.py:409
Async XLA Ops:
  1.9 0.7 copy-start

commit v4 on v3

--- a/solution.py
+++ b/solution.py
@@ -20,7 +20,7 @@
 WIDE = MEM + ROWS
 HALF = 256
 AHEAD = 2
-VLIMIT = 48
+VLIMIT = 46
 MASKED = -1e30
 SCALING = 1.0 / math.sqrt(HEAD)
 LOG2_SCALING = SCALING * math.log2(math.e)
@@ -30,11 +30,11 @@
 
 def kernel(
     depth,
-    q_ref, k_ref, v_ref, g_ref, bias_ref, length_ref, end_ref,
+    q_ref, k_ref, v_ref, g_ref, bias_hbm, length_ref, end_ref,
     o_ref, gq_ref, gk_ref, gv_ref, gb_ref,
     q_buf, g_buf, k_buf, v_buf, o_buf, gq_buf, gk_buf, gv_buf,
-    k_relay, v_relay, info, mask, part_bias, z_bias, y_bias, sum_bias,
-    in_send, in_recv, mem_send, mem_recv, relay_send, relay_recv, out_send, out_recv, info_sem, z_sem, z_recv, y_sem, y_recv, hello,
+    bias_ref, k_relay, v_relay, info, mask, part_bias, z_bias, y_bias, sum_bias,
+    in_send, in_recv, mem_send, mem_recv, relay_send, relay_recv, out_send, out_recv, info_sem, z_sem, z_recv, y_sem, y_recv, hello, small_sem,
 ):
     c, t = lax.axis_index("ctx"), lax.axis_index("tsp")
     shards = depth * RING * 2
@@ -61,6 +61,9 @@
     onward_from = place(z - jnp.where((y == 0) | (y == 1), 1, 0), y + 1)
 
     x_peers = [(dk, dt) for dt in (1, 2, 3) for dk in (0, 1)] + [(1, 0)]
+
+    fetch = pltpu.make_async_copy(bias_hbm, bias_ref, small_sem)
+    fetch.start()
 
     barrier = pltpu.get_barrier_semaphore()
 
@@ -147,6 +150,8 @@
         return carry
 
     lax.fori_loop(0, AHEAD, first_sends, 0)
+
+    fetch.wait()
 
     usable = jnp.minimum(length_ref[0], c * ROWS)
     tile_row = lax.broadcasted_iota(jnp.int32, (8, 128), 0)
@@ -360,15 +365,19 @@
 
     def step(queries, keys, values, cotangent, content_bias, memory_lengths, segment_ends):
         any_spec = pl.BlockSpec(memory_space=pl.ANY)
+        smem_spec = pl.BlockSpec(memory_space=pltpu.SMEM)
         vmem_spec = pl.BlockSpec(memory_space=pltpu.VMEM)
-        smem_spec = pl.BlockSpec(memory_space=pltpu.SMEM)
         slab = jax.ShapeDtypeStruct(queries.shape, half)
         dma, vmem = pltpu.SemaphoreType.DMA, pltpu.VMEM
+        in_hbm = [
+            pltpu.with_memory_space_constraint(value, pltpu.HBM)
+            for value in (queries, keys, values, cotangent, content_bias)
+        ]
         found = pl.pallas_call(
             functools.partial(kernel, depth),
-            out_shape=(slab, slab, slab, slab, jax.ShapeDtypeStruct(content_bias.shape, jnp.float32)),
-            in_specs=[any_spec] * 4 + [vmem_spec, smem_spec, smem_spec],
-            out_specs=[any_spec] * 4 + [vmem_spec],
+            out_shape=[vmem(queries.shape, half)] * 4 + [vmem(content_bias.shape, jnp.float32)],
+            in_specs=[pl.BlockSpec(memory_space=pltpu.HBM)] * 5 + [smem_spec, smem_spec],
+            out_specs=[vmem_spec] * 5,
             scratch_shapes=[
                 vmem((LOCAL, 2 * ROWS, HEAD), half),
                 vmem((LOCAL, 2 * ROWS, HEAD), half),
@@ -378,6 +387,7 @@
                 vmem((LOCAL, 2 * ROWS, HEAD), half),
                 vmem((LOCAL, 2 * ROWS, HEAD), half),
                 vmem((LOCAL, 2 * ROWS, HEAD), half),
+                vmem(content_bias.shape, jnp.float32),
                 vmem((LOCAL, ROWS, HEAD), half),
                 vmem((LOCAL, ROWS, HEAD), half),
                 vmem((2, 8, 128), jnp.float32),
@@ -400,12 +410,13 @@
                 dma(()),
                 dma((RING,)),
                 pltpu.SemaphoreType.REGULAR,
+                dma(()),
             ],
             compiler_params=pltpu.CompilerParams(
                 collective_id=1, has_side_effects=True, vmem_limit_bytes=VLIMIT * 1024 * 1024
             ),
             cost_estimate=pl.CostEstimate(flops=12 * 10**9, bytes_accessed=20 * 10**6, transcendentals=10**7),
-        )(queries, keys, values, cotangent, content_bias, memory_lengths, segment_ends)
+        )(*in_hbm, memory_lengths, segment_ends)
         return pl.pallas_call(
             write_out,
             out_shape=(slab, slab, slab, slab, jax.ShapeDtypeStruct(content_bias.shape, jnp.float32)),

time: 126 us -> 126 us (level)
  no operation moved by 1% of the time
where the time goes in v4:
time: 126 us; the launch traced here: 125 us
  Pallas kernels  123 us (98%)
  between operations  1.93 us (2%)
    pallas_call x1, Pallas kernels, step(): pl.pallas_call(functools.partial(kernel, depth), out_shape=[vmem(queries....  121 us

profile of v4, /device:TPU:1, one launch (start us, length us, event | category | flops | bytes accessed | tf_op | source)
XLA Modules:
  0.0 125.1 jit_solution(12357954098726924048)
XLA Ops:
  1.9 120.7 %shard_map.110 = (bf16[128,5120]{1,0:T(8,128)(2,1)S(1)}, bf16[128,5120]{1,0:T(8,128)(2,1)S(1)}, bf16[128,5120]{1,0:T(8,128)(2,1)S(1)}, bf16[128,5120]{1,0:T(8,128)(2,1)S(1)}, f32[10,128]{1,0:T(8,128)S(1)}) custom-call(bf16[128,5120]{1,0:T(8,128)(2,1)} %q_ref.1, bf16[128,5120]{1,0:T(8,128)(2,1)} %k_ref.1, bf16[128,5120]{1,0:T(8,128)(2,1)} %v_ref.1, ...), custom_call_target="tpu_custom_call" | custom-call | flops 12000000000 | bytes 20000000 | tf_op jit(solution)/shard_map/pallas_call | solution.py:376
  122.7 2.4 %shard_map.111 = (bf16[128,5120]{1,0:T(8,128)(2,1)}, bf16[128,5120]{1,0:T(8,128)(2,1)}, bf16[128,5120]{1,0:T(8,128)(2,1)}, bf16[128,5120]{1,0:T(8,128)(2,1)}, f32[10,128]{1,0:T(8,128)}) custom-call(bf16[128,5120]{1,0:T(8,128)(2,1)S(1)} %get-tuple-element.10.o_in, bf16[128,5120]{1,0:T(8,128)(2,1)S(1)} %get-tuple-element.11.gq_in, ...), custom_call_target="tpu_custom_call" | custom-call | tf_op jit(solution)/shard_map/pallas_call | solution.py:420

commit v5 on v4

--- a/solution.py
+++ b/solution.py
@@ -184,7 +184,7 @@
     def gather_step(head, carry):
         wait_in((0, 1), head)
 
-        @pl.when(head < 2)
+        @pl.when(head < 3)
         def _():
             send_memory(head)
 
@@ -272,9 +272,9 @@
     def head_step(head, carry):
         wait_memory(head)
 
-        @pl.when(head < LOCAL - 2)
-        def _():
-            send_memory(head + 2)
+        @pl.when(head < LOCAL - 3)
+        def _():
+            send_memory(head + 3)
 
         wait_in((2, 3), head)
 

time: 126 us -> 125 us (level)
  no operation moved by 1% of the time
where the time goes in v5:
time: 125 us
  Pallas kernels  123 us (98%)
  between operations  1.93 us (2%)
    pallas_call x1, Pallas kernels, step(): pl.pallas_call(functools.partial(kernel, depth), out_shape=[vmem(queries....  121 us

profile of v5, /device:TPU:1, one launch (start us, length us, event | category | flops | bytes accessed | tf_op | source)
XLA Modules:
  0.0 125.1 jit_solution(9329454197033370808)
XLA Ops:
  1.9 120.7 %shard_map.110 = (bf16[128,5120]{1,0:T(8,128)(2,1)S(1)}, bf16[128,5120]{1,0:T(8,128)(2,1)S(1)}, bf16[128,5120]{1,0:T(8,128)(2,1)S(1)}, bf16[128,5120]{1,0:T(8,128)(2,1)S(1)}, f32[10,128]{1,0:T(8,128)S(1)}) custom-call(bf16[128,5120]{1,0:T(8,128)(2,1)} %q_ref.1, bf16[128,5120]{1,0:T(8,128)(2,1)} %k_ref.1, bf16[128,5120]{1,0:T(8,128)(2,1)} %v_ref.1, ...), custom_call_target="tpu_custom_call" | custom-call | flops 12000000000 | bytes 20000000 | tf_op jit(solution)/shard_map/pallas_call | solution.py:376
  122.7 2.4 %shard_map.111 = (bf16[128,5120]{1,0:T(8,128)(2,1)}, bf16[128,5120]{1,0:T(8,128)(2,1)}, bf16[128,5120]{1,0:T(8,128)(2,1)}, bf16[128,5120]{1,0:T(8,128)(2,1)}, f32[10,128]{1,0:T(8,128)}) custom-call(bf16[128,5120]{1,0:T(8,128)(2,1)S(1)} %get-tuple-element.10.o_in, bf16[128,5120]{1,0:T(8,128)(2,1)S(1)} %get-tuple-element.11.gq_in, ...), custom_call_target="tpu_custom_call" | custom-call | tf_op jit(solution)/shard_map/pallas_call | solution.py:420
